TPU v7x, 32 devices: a whole 2x2x4 slice. The times are simulated.
32 devices in a mesh: tm: 8 (over z, core), row: 2 (over x), col: 2 (over y).
Axes of the slice: x: 2, y: 2, z: 4, core: 2. Of those that a mesh axis runs over, the one named last changes fastest.
Arguments:
- latents: bfloat16 [16, 64, 10240], P('tm', 'row', 'col'), may hold values from -6 to 6
- w_qkv: bfloat16 [320, 960], replicated, may hold values from -4 to 4
- w_out: bfloat16 [320, 320], replicated, may hold values from -0.3125 to 0.3125
- conv_weight: float32 [9, 320], replicated, may hold values from -1.8 to 1.8
Outputs:
- result: bfloat16 [16, 64, 10240], P('tm', 'row', 'col')
All inputs are finite; a program needn't handle non-finite values.
Results may differ from a plain program's by a relative error of at most 0.013.
Values may be sent and summed in bfloat16 or wider, within the bound.
A program may use at most 64 MiB of HBM per device.

v0:
```python
import jax
import jax.numpy as jnp
from jax import lax
from jax.sharding import PartitionSpec as P

HEAD_DIM = 64


def padded_2(cells, sides, width):
    for axis, dim in sides:
        count = lax.axis_size(axis)
        ends = count - 1
        head = lax.slice_in_dim(cells, 0, width, axis=dim)
        tail = lax.slice_in_dim(cells, cells.shape[dim] - width, cells.shape[dim], axis=dim)
        cells = jnp.concatenate(
            [
                lax.ppermute(tail, axis, [(i, (i + 1) % count) for i in range(ends)]),
                cells,
                lax.ppermute(head, axis, [((i + 1) % count, i) for i in range(ends)]),
            ],
            axis=dim,
        )
    return cells


def layer_norm(flat):
    mean = jnp.mean(flat, axis=-1, keepdims=True)
    cent = flat - mean
    var = jnp.mean(cent * cent, axis=-1, keepdims=True)
    return (cent * lax.rsqrt(var + 1e-05)).astype(jnp.bfloat16)


def body(latents, w_qkv, w_out, conv_weight):
    frames, rows, merged = latents.shape
    chans = w_out.shape[0]
    cols = merged // chans
    points = rows * cols
    flat = latents.reshape(frames * points, chans).astype(jnp.float32)
    normed = layer_norm(flat)
    query = jnp.dot(normed, w_qkv[:, :chans], preferred_element_type=jnp.float32).astype(
        jnp.bfloat16
    )
    query = query.reshape(frames, points, chans)
    keys_own = jnp.dot(
        normed, w_qkv[:, chans : 2 * chans], preferred_element_type=jnp.float32
    ).astype(jnp.bfloat16)
    vals_own = jnp.dot(normed, w_qkv[:, 2 * chans :], preferred_element_type=jnp.float32).astype(
        jnp.bfloat16
    )
    stacked_kv = jnp.stack(
        [keys_own.reshape(frames, points, chans), vals_own.reshape(frames, points, chans)], 0
    )
    wide = padded_2(stacked_kv, (("tm", 1),), 2)
    first = lax.axis_index("tm") * frames
    total = lax.axis_size("tm") * frames
    group = jnp.arange(chans, dtype=jnp.int32) // HEAD_DIM
    head_sum = (group[:, None] == group[None, :]).astype(jnp.float32)
    scale = HEAD_DIM ** (-0.5)
    q_wide = query.astype(jnp.float32)
    scores = []
    for shift_d in range(5):
        prod = q_wide * wide[0, shift_d : shift_d + frames].astype(jnp.float32)
        score = jnp.dot(
            prod.reshape(frames * points, chans), head_sum, precision=lax.Precision.HIGHEST
        )
        score = score.reshape(frames, points, chans) * scale
        where_t = first + jnp.arange(frames, dtype=jnp.int32) + (shift_d - 2)
        valid = (where_t >= 0) & (where_t < total)
        scores.append(jnp.where(valid[:, None, None], score, jnp.float32(-1e30)))
    stacked = jnp.stack(scores, 0)
    top = jnp.max(stacked, axis=0, keepdims=True)
    expo = jnp.exp(stacked - top)
    weights = (expo / jnp.sum(expo, axis=0, keepdims=True)).astype(jnp.bfloat16)
    mixed = jnp.zeros((frames, points, chans), jnp.float32)
    for shift_d in range(5):
        mixed = mixed + weights[shift_d].astype(jnp.float32) * wide[
            1, shift_d : shift_d + frames
        ].astype(jnp.float32)
    attended = mixed.astype(jnp.bfloat16).reshape(frames * points, chans)
    proj = jnp.dot(attended, w_out, preferred_element_type=jnp.float32)
    hidden = (flat + proj).astype(jnp.bfloat16).reshape(frames, rows, cols * chans)
    tall = padded_2(hidden, (("row", 1),), 1)
    padded = padded_2(tall, (("col", 2),), chans)
    taps = jnp.tile(conv_weight, (1, cols))
    acc = hidden.astype(jnp.float32)
    span = cols * chans
    for tap_a in range(3):
        for tap_b in range(3):
            acc = (
                acc
                + padded[:, tap_a : tap_a + rows, tap_b * chans : tap_b * chans + span].astype(
                    jnp.float32
                )
                * taps[3 * tap_a + tap_b]
            )
    return acc.astype(jnp.bfloat16)


def solution(mesh):
    placed = (P("tm", "row", "col"), P(), P(), P())
    return jax.shard_map(
        body, mesh=mesh, in_specs=placed, out_specs=P("tm", "row", "col"), check_vma=False
    )
```

profile of v0, /device:TPU:10, one launch (start us, length us, event | category | flops | bytes accessed | tf_op | source)
XLA Modules:
  0.0 88.6 jit_solution(14240052632750793772)
XLA Ops:
  0.0 1.7 %reshape.198 = f32[1024,320]{1,0:T(8,128)S(1)} reshape(bf16[2,32,5120]{2,1,0:T(8,128)(2,1)} %param.4) | data formatting | bytes 1966080 | tf_op jit(solution)/shard_map/convert_element_type | solution.py:38
  4.0 1.4 %convolution_convert_fusion = bf16[1024,320]{0,1:T(8,128)(2,1)} fusion(bf16[1024,320]{1,0:T(8,128)(2,1)S(1)} %multiply_convert_fusion, bf16[320,960]{1,0:T(8,128)(2,1)S(1)} %copy-done.4), kind=kOutput, calls=%fused_computation.24 | convolution fusion | flops 210042880 | bytes 1687552 | tf_op jit(solution)/shard_map/dot_general | solution.py:47
  6.8 2.0 %copy_dynamic-update-slice_fusion.1 = bf16[2,2,512,320]{2,3,1,0:T(8,128)(2,1)} fusion(bf16[1,2,512,320]{2,1,3,0:T(2,128)(2,1)} %stack_reshape.6), kind=kLoop, calls=%fused_computation.68 | loop fusion | bytes 1310720
  8.8 3.0 %stack_reshape.7 = bf16[1,2,512,320]{2,1,3,0:T(2,128)(2,1)} reshape(bf16[1024,320]{0,1:T(8,128)(2,1)} %convolution_convert_fusion) | data formatting | bytes 1310720 | tf_op jit(solution)/shard_map/stack;reshape | solution.py:50
  11.7 2.0 %copy_dynamic-update-slice_fusion = bf16[2,2,512,320]{2,3,1,0:T(8,128)(2,1)} fusion(bf16[2,2,512,320]{2,3,1,0:T(8,128)(2,1)} %copy_dynamic-update-slice_fusion.1, bf16[1,2,512,320]{2,1,3,0:T(2,128)(2,1)} %stack_reshape.7), kind=kLoop, calls=%fused_computation.67 | loop fusion | bytes 1310720 | tf_op jit(solution)/shard_map/stack | solution.py:50
  13.7 1.9 %collective-permute-start = (bf16[2,2,512,320]{2,3,1,0:T(8,128)(2,1)}, bf16[2,2,512,320]{2,3,1,0:T(8,128)(2,1)}, u32[]{:S(2)}, u32[]{:S(2)}) collective-permute-start(bf16[2,2,512,320]{2,3,1,0:T(8,128)(2,1)} %copy_dynamic-update-slice_fusion), channel_id=1, source_target_pairs={{0,4},{4,8},{8,12},{12,16},{16,20},{20,24},{24,28},{1,5},{5,9},{9,... | collective-permute-start | bytes 3932168 | tf_op jit(solution)/shard_map/ppermute | solution.py:17
  15.7 3.8 %collective-permute-start.1 = (bf16[2,2,512,320]{2,3,1,0:T(8,128)(2,1)}, bf16[2,2,512,320]{2,3,1,0:T(8,128)(2,1)}, u32[]{:S(2)}, u32[]{:S(2)}) collective-permute-start(bf16[2,2,512,320]{2,3,1,0:T(8,128)(2,1)} %copy_dynamic-update-slice_fusion), channel_id=1, source_target_pairs={{4,0},{8,4},{12,8},{16,12},{20,16},{24,20},{28,24},{5,1},{9,5},{13... | collective-permute-start | bytes 3932168 | tf_op jit(solution)/shard_map/ppermute | solution.py:19
  19.5 1.5 %copy.35 = f32[1024,320]{0,1:T(8,128)} copy(f32[1024,320]{1,0:T(8,128)S(1)} %reshape.198) | data formatting | bytes 2621440 | tf_op jit(solution)/shard_map/convert_element_type | solution.py:38
  21.1 11.9 %collective-permute-done = bf16[2,2,512,320]{2,3,1,0:T(8,128)(2,1)} collective-permute-done((bf16[2,2,512,320]{2,3,1,0:T(8,128)(2,1)}, bf16[2,2,512,320]{2,3,1,0:T(8,128)(2,1)}, u32[]{:S(2)}, u32[]{:S(2)}) %collective-permute-start) | collective-permute-done | bytes 1310752 | tf_op jit(solution)/shard_map/ppermute | solution.py:17
  33.0 1.8 %collective-permute-done.1 = bf16[2,2,512,320]{2,3,1,0:T(8,128)(2,1)} collective-permute-done((bf16[2,2,512,320]{2,3,1,0:T(8,128)(2,1)}, bf16[2,2,512,320]{2,3,1,0:T(8,128)(2,1)}, u32[]{:S(2)}, u32[]{:S(2)}) %collective-permute-start.1) | collective-permute-done | bytes 1310752 | tf_op jit(solution)/shard_map/ppermute | solution.py:19
  34.7 2.4 %slice_convert_fusion.1 = (f32[1,2,512,320]{2,3,1,0:T(8,128)S(1)}, f32[1,2,512,320]{2,3,1,0:T(8,128)S(1)}, f32[1,2,512,320]{2,3,1,0:T(8,128)S(1)}, f32[1,2,512,320]{2,3,1,0:T(8,128)S(1)}) fusion(bf16[2,2,512,320]{2,3,1,0:T(8,128)(2,1)} %collective-permute-done.1, bf16[2,2,512,320]{2,3,1,0:T(8,128)(2,1)} %copy_dynamic-update-slice_fusion, ...), kind=kLoop, calls=%fused_computation.63 | loop fusion | flops 1966080 | bytes 10485760 | tf_op jit(solution)/shard_map/convert_element_type | solution.py:62
  42.3 1.8 %convert_multiply_fusion = (f32[1024,320]{0,1:T(8,128)S(1)}, f32[1024,320]{0,1:T(8,128)S(1)}, f32[1024,320]{0,1:T(8,128)S(1)}, f32[1024,320]{0,1:T(8,128)S(1)}, f32[1024,320]{0,1:T(8,128)S(1)}) fusion(f32[1024,320]{0,1:T(8,128)S(1)} %bitcast.114, f32[1024,320]{0,1:T(8,128)S(1)} %bitcast.115, bf16[1024,320]{0,1:T(8,128)(2,1)S(1)} %convolution_convert_fusion.1, ...), kind=kOutput, calls=%fused_computation.3 | convolution fusion | flops 212336640 | bytes 13352960 | tf_op jit(solution)/shard_map/dot_general | solution.py:40
  44.2 1.4 %bitcast_dynamic-update-slice_fusion.4 = (f32[5,2,512,320]{2,3,1,0:T(8,128)S(1)}, f32[2,512,320]{1,2,0:T(8,128)S(1)}) fusion(s32[320]{0:T(512)S(1)} %add_select_fusion, f32[40,2,8,512]{3,2,1,0:T(8,128)S(1)} %bitcast.113, pred[2]{0:T(512)(128)(4,1)S(1)} %compare_and_fusion.4), kind=kOutput, calls=%fused_computation.50 | convolution fusion | flops 1259048960 | bytes 3936768 | tf_op jit(solution)/shard_map/dot_general | solution.py:63
  45.5 1.3 %bitcast_dynamic-update-slice_fusion.3 = (f32[5,2,512,320]{2,3,1,0:T(8,128)S(1)}, f32[2,512,320]{1,2,0:T(8,128)S(1)}) fusion(f32[5,2,512,320]{2,3,1,0:T(8,128)S(1)} %get-tuple-element.32, s32[320]{0:T(512)S(1)} %add_select_fusion, f32[40,2,8,512]{3,2,1,0:T(8,128)S(1)} %bitcast.112, pred[2]{0:T(512)(128)(4,1)S(1)} %get-tuple-element.45), kind=kOutput, calls=%fused_computation.49 | convolution fusion | flops 1259048960 | bytes 3936768 | tf_op jit(solution)/shard_map/dot_general | solution.py:63
  46.9 1.3 %bitcast_dynamic-update-slice_fusion.2 = (f32[5,2,512,320]{2,3,1,0:T(8,128)S(1)}, f32[2,512,320]{1,2,0:T(8,128)S(1)}) fusion(f32[5,2,512,320]{2,3,1,0:T(8,128)S(1)} %get-tuple-element.34, s32[320]{0:T(512)S(1)} %add_select_fusion, f32[40,2,8,512]{3,2,1,0:T(8,128)S(1)} %bitcast.111, pred[2]{0:T(512)(128)(4,1)S(1)} %get-tuple-element.44), kind=kOutput, calls=%fused_computation.48 | convolution fusion | flops 1259048960 | bytes 3936768 | tf_op jit(solution)/shard_map/dot_general | solution.py:63
  48.2 1.6 %bitcast_dynamic-update-slice_fusion.1 = (f32[5,2,512,320]{2,3,1,0:T(8,128)S(1)}, f32[2,512,320]{1,2,0:T(8,128)S(1)}) fusion(f32[5,2,512,320]{2,3,1,0:T(8,128)S(1)} %get-tuple-element.36, s32[320]{0:T(512)S(1)} %add_select_fusion, f32[40,2,8,512]{3,2,1,0:T(8,128)S(1)} %bitcast.110, pred[2]{0:T(512)(128)(4,1)S(1)} %get-tuple-element.43), kind=kOutput, calls=%fused_computation.47 | convolution fusion | flops 1259048960 | bytes 3936768 | tf_op jit(solution)/shard_map/dot_general | solution.py:63
  52.0 1.4 %fusion = f32[2,512,320]{1,2,0:T(8,128)S(1)} fusion(f32[5,2,512,320]{2,3,1,0:T(8,128)S(1)} %get-tuple-element.40, f32[2,512,320]{1,2,0:T(8,128)S(1)} %maximum_maximum_fusion), kind=kLoop, calls=%fused_computation.2 | loop fusion | flops 2949120 | bytes 9175040 | tf_op jit(solution)/shard_map/reduce_sum | solution.py:73
  53.3 1.7 %divide_convert_fusion = bf16[5,2,512,320]{2,3,1,0:T(8,128)(2,1)S(1)} fusion(f32[5,2,512,320]{2,3,1,0:T(8,128)S(1)} %get-tuple-element.40, f32[2,512,320]{1,2,0:T(8,128)S(1)} %fusion, f32[2,512,320]{1,2,0:T(8,128)S(1)} %maximum_maximum_fusion), kind=kLoop, calls=%fused_computation | loop fusion | flops 4915200 | bytes 12451840 | tf_op jit(solution)/shard_map/convert_element_type | solution.py:73
  56.4 2.1 %multiply_add_fusion = (f32[1,2,512,320]{2,3,1,0:T(8,128)S(1)}, f32[1,2,512,320]{2,3,1,0:T(8,128)S(1)}, f32[1,2,512,320]{2,3,1,0:T(8,128)S(1)}) fusion(bf16[2,2,512,320]{2,3,1,0:T(8,128)(2,1)S(1)} %copy-done.1, bf16[2,2,512,320]{2,3,1,0:T(8,128)(2,1)} %collective-permute-done, bf16[5,2,512,320]{2,3,1,0:T(8,128)(2,1)S(1)} %divide_convert_fusion, ...), kind=kLoop, calls=%fused_computation.54 | loop fusion | flops 4915200 | bytes 11796480 | tf_op jit(solution)/shard_map/add | solution.py:76
  67.0 2.4 %collective-permute-start.3 = (bf16[2,1,5120]{2,1,0:T(2,128)(2,1)S(1)}, bf16[2,1,5120]{2,1,0:T(2,128)(2,1)S(1)}, u32[]{:S(2)}, u32[]{:S(2)}) collective-permute-start(bf16[2,1,5120]{2,1,0:T(2,128)(2,1)S(1)} %get-tuple-element.26), channel_id=1, source_target_pairs={{2,0},{3,1},{6,4},{7,5},{10,8},{11,9},{14,12},{15,13},{18,16},{19,... | collective-permute-start | bytes 61448 | tf_op jit(solution)/shard_map/ppermute | solution.py:19
  71.1 4.2 %collective-permute-done.2 = bf16[2,1,5120]{2,1,0:T(2,128)(2,1)S(1)} collective-permute-done((bf16[2,1,5120]{2,1,0:T(2,128)(2,1)S(1)}, bf16[2,1,5120]{2,1,0:T(2,128)(2,1)S(1)}, u32[]{:S(2)}, u32[]{:S(2)}) %collective-permute-start.2) | collective-permute-done | bytes 20512 | tf_op jit(solution)/shard_map/ppermute | solution.py:17
  75.4 3.4 %collective-permute-start.4 = (bf16[2,34,320]{2,1,0:T(8,128)(2,1)S(1)}, bf16[2,34,320]{2,1,0:T(8,128)(2,1)S(1)}, u32[]{:S(2)}, u32[]{:S(2)}) collective-permute-start(bf16[2,34,320]{2,1,0:T(8,128)(2,1)S(1)} %get-tuple-element.23), channel_id=1, source_target_pairs={{0,1},{2,3},{4,5},{6,7},{8,9},{10,11},{12,13},{14,15},{16,17},{18,... | collective-permute-start | bytes 130568 | tf_op jit(solution)/shard_map/ppermute | solution.py:17
  81.0 4.0 %collective-permute-done.5 = bf16[2,34,320]{2,1,0:T(8,128)(2,1)S(1)} collective-permute-done((bf16[2,34,320]{2,1,0:T(8,128)(2,1)S(1)}, bf16[2,34,320]{2,1,0:T(8,128)(2,1)S(1)}, u32[]{:S(2)}, u32[]{:S(2)}) %collective-permute-start.5) | collective-permute-done | bytes 43552 | tf_op jit(solution)/shard_map/ppermute | solution.py:19
  85.7 2.8 %fusion.15 = bf16[2,32,5120]{2,1,0:T(8,128)(2,1)} fusion(bf16[2,32,5120]{2,1,0:T(8,128)(2,1)S(1)} %reshape.197, bf16[2,34,5440]{2,1,0:T(8,128)(2,1)S(1)} %get-tuple-element.22, bf16[2,1,5120]{2,1,0:T(2,128)(2,1)S(1)} %collective-permute-done.3, bf16[2,34,5440]{2,1,0:T(8,128)(2,1)S(1)} %get-tuple-element.21, ...), kind=kLoop, calls=%fused_computation.35 | loop fusion | flops 11141120 | bytes 5468160 | tf_op jit(solution)/shard_map/convert_element_type | solution.py:96
  (71 shorter events, 25.1 us)
Async XLA Ops:
  0.0 63.7 %copy-start = (bf16[320,320]{1,0:T(8,128)(2,1)S(1)}, bf16[320,320]{1,0:T(8,128)(2,1)}, u32[]{:S(2)}) copy-start(bf16[320,320]{1,0:T(8,128)(2,1)} %param.6) | copy-start | bytes 614404
  2.3 1.1 %copy-start.4 = (bf16[320,960]{1,0:T(8,128)(2,1)S(1)}, bf16[320,960]{1,0:T(8,128)(2,1)}, u32[]{:S(2)}) copy-start(bf16[320,960]{1,0:T(8,128)(2,1)} %param.5) | copy-start | bytes 1843204
  13.7 19.2 %collective-permute-start = (bf16[2,2,512,320]{2,3,1,0:T(8,128)(2,1)}, bf16[2,2,512,320]{2,3,1,0:T(8,128)(2,1)}, u32[]{:S(2)}, u32[]{:S(2)}) collective-permute-start(bf16[2,2,512,320]{2,3,1,0:T(8,128)(2,1)} %copy_dynamic-update-slice_fusion), channel_id=1, source_target_pairs={{0,4},{4,8},{8,12},{12,16},{16,20},{20,24},{24,28},{1,5},{5,9},{9,... | collective-permute-start | bytes 3932168 | tf_op jit(solution)/shard_map/ppermute | solution.py:17
  15.7 19.1 %collective-permute-start.1 = (bf16[2,2,512,320]{2,3,1,0:T(8,128)(2,1)}, bf16[2,2,512,320]{2,3,1,0:T(8,128)(2,1)}, u32[]{:S(2)}, u32[]{:S(2)}) collective-permute-start(bf16[2,2,512,320]{2,3,1,0:T(8,128)(2,1)} %copy_dynamic-update-slice_fusion), channel_id=1, source_target_pairs={{4,0},{8,4},{12,8},{16,12},{20,16},{24,20},{28,24},{5,1},{9,5},{13... | collective-permute-start | bytes 3932168 | tf_op jit(solution)/shard_map/ppermute | solution.py:19
  55.0 1.3 %copy-start.1 = (bf16[2,2,512,320]{2,3,1,0:T(8,128)(2,1)S(1)}, bf16[2,2,512,320]{2,3,1,0:T(8,128)(2,1)}, u32[]{:S(2)}) copy-start(bf16[2,2,512,320]{2,3,1,0:T(8,128)(2,1)} %copy_dynamic-update-slice_fusion) | copy-start | bytes 3932164
  63.4 1.1 %copy-start.2 = (bf16[1024,320]{0,1:T(8,128)(2,1)S(1)}, bf16[1024,320]{0,1:T(8,128)(2,1)}, u32[]{:S(2)}) copy-start(bf16[1024,320]{0,1:T(8,128)(2,1)} %convolution_convert_fusion) | copy-start | bytes 1966084
  63.4 1.5 %copy-start.3 = (f32[1024,320]{0,1:T(8,128)S(1)}, f32[1024,320]{0,1:T(8,128)}, u32[]{:S(2)}) copy-start(f32[1024,320]{0,1:T(8,128)} %copy.35) | copy-start | bytes 3932164
  66.2 13.9 %copy-start.5 = (f32[9,320]{1,0:T(8,128)S(1)}, f32[9,320]{1,0:T(8,128)}, u32[]{:S(2)}) copy-start(f32[9,320]{1,0:T(8,128)} %param.7) | copy-start | bytes 34564
  67.0 4.1 %collective-permute-start.3 = (bf16[2,1,5120]{2,1,0:T(2,128)(2,1)S(1)}, bf16[2,1,5120]{2,1,0:T(2,128)(2,1)S(1)}, u32[]{:S(2)}, u32[]{:S(2)}) collective-permute-start(bf16[2,1,5120]{2,1,0:T(2,128)(2,1)S(1)} %get-tuple-element.26), channel_id=1, source_target_pairs={{2,0},{3,1},{6,4},{7,5},{10,8},{11,9},{14,12},{15,13},{18,16},{19,... | collective-permute-start | bytes 61448 | tf_op jit(solution)/shard_map/ppermute | solution.py:19
  69.4 5.9 %collective-permute-start.2 = (bf16[2,1,5120]{2,1,0:T(2,128)(2,1)S(1)}, bf16[2,1,5120]{2,1,0:T(2,128)(2,1)S(1)}, u32[]{:S(2)}, u32[]{:S(2)}) collective-permute-start(bf16[2,1,5120]{2,1,0:T(2,128)(2,1)S(1)} %get-tuple-element.25), channel_id=1, source_target_pairs={{0,2},{1,3},{4,6},{5,7},{8,10},{9,11},{12,14},{13,15},{16,18},{17,... | collective-permute-start | bytes 61448 | tf_op jit(solution)/shard_map/ppermute | solution.py:17
  75.4 5.6 %collective-permute-start.4 = (bf16[2,34,320]{2,1,0:T(8,128)(2,1)S(1)}, bf16[2,34,320]{2,1,0:T(8,128)(2,1)S(1)}, u32[]{:S(2)}, u32[]{:S(2)}) collective-permute-start(bf16[2,34,320]{2,1,0:T(8,128)(2,1)S(1)} %get-tuple-element.23), channel_id=1, source_target_pairs={{0,1},{2,3},{4,5},{6,7},{8,9},{10,11},{12,13},{14,15},{16,17},{18,... | collective-permute-start | bytes 130568 | tf_op jit(solution)/shard_map/ppermute | solution.py:17
  78.9 6.1 %collective-permute-start.5 = (bf16[2,34,320]{2,1,0:T(8,128)(2,1)S(1)}, bf16[2,34,320]{2,1,0:T(8,128)(2,1)S(1)}, u32[]{:S(2)}, u32[]{:S(2)}) collective-permute-start(bf16[2,34,320]{2,1,0:T(8,128)(2,1)S(1)} %get-tuple-element.24), channel_id=1, source_target_pairs={{1,0},{3,2},{5,4},{7,6},{9,8},{11,10},{13,12},{15,14},{17,16},{19,... | collective-permute-start | bytes 130568 | tf_op jit(solution)/shard_map/ppermute | solution.py:19
where the time goes:
time: 89.1 us; the launch traced here: 88.6 us
  local copies, waits for them, and re-layouts  26.7 us (30%)
  waiting for transfers between devices  22.3 us (25%)
  starting transfers between devices  14.2 us (16%)
  other arithmetic  13.3 us (15%)
  matrix products  11.7 us (13%)
    ppermute x3, waiting for transfers between devices, padded_2(): lax.ppermute(tail, axis, [(i, (i + 1) % count) for i in range(ends)])  16.2 us
    ppermute x3, starting transfers between devices, padded_2(): lax.ppermute(head, axis, [((i + 1) % count, i) for i in range(ends)])  7.56 us
    unnamed x21, local copies, waits for them, and re-layouts  7.24 us
    dot_general x5, matrix products, body(): jnp.dot(prod.reshape(frames * points, chans), head_sum, precision=lax.Pre...  6.95 us
    ppermute x3, starting transfers between devices, padded_2(): lax.ppermute(tail, axis, [(i, (i + 1) % count) for i in range(ends)])  6.64 us
    another operation x3, local copies, waits for them, and re-layouts, body(): jnp.stack([keys_own.reshape(frames, points, chans), vals_own.reshape(fram...  6.27 us
    ppermute x3, waiting for transfers between devices, padded_2(): lax.ppermute(head, axis, [((i + 1) % count, i) for i in range(ends)])  6.1 us
    convert_element_type x4, local copies, waits for them, and re-layouts, body(): prod = q_wide * wide[0, shift_d:shift_d + frames].astype(jnp.float32)  4.05 us
  transfers between devices with their start and end apart: 6, of which 5 were waited for; matrix products, arithmetic and copies ran while one was open for 3% of the time, Pallas kernels for 0%

commit v1 on v0

v1 whole, which is shorter than its diff:
```python
import functools

import jax
import jax.numpy as jnp
from jax import lax
from jax.experimental import pallas as pl
from jax.experimental.pallas import tpu as pltpu
from jax.sharding import PartitionSpec as P

HEAD_DIM = 64
LOG2E = 1.4426950408889634
MESH = pl.DeviceIdType.MESH
F32, BF16 = jnp.float32, jnp.bfloat16


def dot(a, b):
    return jnp.dot(a, b, preferred_element_type=F32)


def widen(even, odd, lane):
    mid = jnp.where(lane < 64, even, odd)
    return jnp.concatenate([even, even, mid, odd, odd], axis=1)


def kernel(
    sizes,
    x_ref, wqkv_ref, wout_ref, cw_ref, out_ref,
    norm, q_s, k_s, v_s, hid, swp, rowf, rows_out, rows_in, corn_in, edge,
    w1q, w2q, w3q, w1kv, w2kv, w3kv, w1o, w2o, w3o, taps, ones2, heads,
    t_send, t_recv, c_send, c_recv, r_send, r_recv, d_send, d_recv,
):
    n_t, n_r, n_c = sizes
    frames, rows, merged = x_ref.shape
    chans = wout_ref.shape[0]
    wide = 2 * chans
    pairs = merged // wide
    fr = frames * rows
    me_t, me_r, me_c = lax.axis_index("tm"), lax.axis_index("row"), lax.axis_index("col")

    has_t = (me_t > 0, me_t < n_t - 1)
    has_r = (me_r > 0, me_r < n_r - 1)
    has_c = (me_c > 0, me_c < n_c - 1)
    step = (-1, 1)
    near = []
    for s in range(2):
        near.append((has_t[s], (me_t + step[s], me_r, me_c)))
        near.append((has_r[s], (me_t, me_r + step[s], me_c)))
        near.append((has_c[s], (me_t, me_r, me_c + step[s])))
    diag = []
    for s in range(2):
        for u in range(2):
            diag.append(
                (has_r[s] & has_c[u], (me_t, me_r + step[s], me_c + step[u]), 2 * s + u)
            )
    barrier = pltpu.get_barrier_semaphore()
    count = jnp.int32(0)
    for ok, where in near + [d[:2] for d in diag]:
        @pl.when(ok)
        def _():
            pl.semaphore_signal(barrier, inc=1, device_id=where, device_id_type=MESH)
        count = count + jnp.where(ok, 1, 0).astype(jnp.int32)

    lane = lax.broadcasted_iota(jnp.int32, (1, 128), 1)

    at = lax.broadcasted_iota(jnp.int32, (wide, 256), 0)
    to = lax.broadcasted_iota(jnp.int32, (wide, 256), 1)
    ones2[...] = jnp.where((at < chans) == (to < 128), 1.0, 0.0).astype(BF16)
    at = lax.broadcasted_iota(jnp.int32, (256, 256), 0) // HEAD_DIM
    to = lax.broadcasted_iota(jnp.int32, (256, 256), 1) // HEAD_DIM
    heads[...] = jnp.where(at == to, 1.0, 0.0).astype(BF16)

    for s in range(2):
        @pl.when(jnp.logical_not(has_t[s]))
        def _():
            norm[:, s] = jnp.zeros((pairs, fr, wide), BF16)
        @pl.when(jnp.logical_not(has_c[s]))
        def _():
            swp[0 if s == 0 else pairs + 1] = jnp.zeros((fr, wide), BF16)
        @pl.when(jnp.logical_not(has_r[s]))
        def _():
            rows_in[s] = jnp.zeros(rows_in.shape[1:], BF16)
    for ok, _, i in diag:
        @pl.when(jnp.logical_not(ok))
        def _():
            corn_in[i] = jnp.zeros(corn_in.shape[1:], BF16)

    pl.semaphore_wait(barrier, count)

    def t_copy(s, p):
        return pltpu.make_async_remote_copy(
            src_ref=norm.at[p, 2], dst_ref=norm.at[p, 1 - s],
            send_sem=t_send.at[s, p], recv_sem=t_recv.at[1 - s, p],
            device_id=(me_t + step[s], me_r, me_c), device_id_type=MESH,
        )

    def normalise(p, carry):
        xb = x_ref[:, :, pl.ds(pl.multiple_of(p * wide, 128), wide)].reshape(fr, wide)
        sums = dot(xb, ones2[...]) * (1.0 / chans)
        cent = xb.astype(F32) - widen(sums[:, :128], sums[:, 128:], lane)
        var = dot((cent * cent).astype(BF16), ones2[...]) * (1.0 / chans)
        inv = lax.rsqrt(var + 1e-05)
        norm[p, 2] = (cent * widen(inv[:, :128], inv[:, 128:], lane)).astype(BF16)
        for s in range(2):
            @pl.when(has_t[s])
            def _():
                t_copy(s, p).start()
        return carry

    lax.fori_loop(0, pairs, normalise, 0)

    pad = wide - chans - 256
    def split(w32, r1, r2, r3, lo1, lo2):
        zero = jnp.zeros((chans, 64), F32)
        r1[0:chans, lo1:lo1 + 256] = w32[:, 0:256].astype(BF16)
        r1[chans:chans + pad, lo1:lo1 + 256] = jnp.zeros((pad, 256), BF16)
        r3[0:pad, lo1:lo1 + 256] = jnp.zeros((pad, 256), BF16)
        r3[pad:pad + chans, lo1:lo1 + 256] = w32[:, 64:320].astype(BF16)
        r2[0:chans, lo2:lo2 + 128] = jnp.concatenate([w32[:, 256:320], zero], 1).astype(BF16)
        r2[chans:, lo2:lo2 + 128] = jnp.concatenate([zero, w32[:, 0:64]], 1).astype(BF16)

    split(wqkv_ref[:, 0:chans].astype(F32), w1q, w2q, w3q, 0, 0)
    split(wqkv_ref[:, chans:2 * chans].astype(F32), w1kv, w2kv, w3kv, 0, 0)
    split(wqkv_ref[:, 2 * chans:].astype(F32), w1kv, w2kv, w3kv, 256, 128)
    split(wout_ref[...].astype(F32), w1o, w2o, w3o, 0, 0)
    taps[...] = jnp.concatenate([cw_ref[...], cw_ref[...]], 1)

    def project(a, r1, r2, r3):
        return jnp.concatenate(
            [dot(a[:, 0:384], r1[...]), dot(a, r2[...]), dot(a[:, 256:640], r3[...])], 1
        )

    def keys_values(a):
        o1 = dot(a[:, 0:384], w1kv[...]).astype(BF16)
        o2 = dot(a, w2kv[...]).astype(BF16)
        o3 = dot(a[:, 256:640], w3kv[...]).astype(BF16)
        keys = jnp.concatenate([o1[:, :256], o2[:, :128], o3[:, :256]], 1)
        vals = jnp.concatenate([o1[:, 256:], o2[:, 128:], o3[:, 256:]], 1)
        return keys, vals

    group = 2
    def own(g, carry):
        at = pl.ds(g * group, group)
        a = norm[at, 2].reshape(group * fr, wide)
        q = project(a, w1q, w2q, w3q) * (HEAD_DIM ** -0.5 * LOG2E)
        q_s[at] = q.astype(BF16).reshape(group, fr, wide)
        keys, vals = keys_values(a)
        k_s[at, 2] = keys.reshape(group, fr, wide)
        v_s[at, 2] = vals.reshape(group, fr, wide)
        return carry

    lax.fori_loop(0, pairs // group, own, 0)

    big = jnp.float32(3e38)
    caps = [jnp.where(has_t[s], big, jnp.float32(-1e30)) for s in range(2)]

    def place(w):
        slot = (0, 2, 1)[w // 2]
        return slot, (w % 2) * rows

    def attend(p, carry):
        for s in range(2):
            @pl.when(has_t[s])
            def _():
                t_copy(1 - s, p).wait_recv()
        keys, vals = keys_values(norm[p, 0:2].reshape(2 * fr, wide))
        k_s[p, 0:2] = keys.reshape(2, fr, wide)
        v_s[p, 0:2] = vals.reshape(2, fr, wide)
        outs = []
        for lo, hi in ((0, 256), (256, 512), (512, 640)):
            prods = []
            for f in range(2):
                q = q_s[p, f * rows:(f + 1) * rows, lo:hi]
                for d in range(5):
                    slot, r0 = place(f + d)
                    prods.append(q * k_s[p, slot, r0:r0 + rows, lo:hi])
            scores = dot(jnp.concatenate(prods, 0), heads[:hi - lo, :hi - lo])
            mixes = []
            for f in range(2):
                parts = []
                for d in range(5):
                    i = (f * 5 + d) * rows
                    part = scores[i:i + rows]
                    slot = place(f + d)[0]
                    if slot < 2:
                        part = jnp.minimum(part, caps[slot])
                    parts.append(part)
                top = functools.reduce(jnp.maximum, parts)
                total, mixed = None, None
                for d in range(5):
                    slot, r0 = place(f + d)
                    e = jnp.exp2(parts[d] - top)
                    m = e * v_s[p, slot, r0:r0 + rows, lo:hi].astype(F32)
                    total = e if d == 0 else total + e
                    mixed = m if d == 0 else mixed + m
                mixes.append((mixed / total).astype(BF16))
            outs.append(jnp.concatenate(mixes, 0))
        att = jnp.concatenate(outs, 1)
        xb = x_ref[:, :, pl.ds(pl.multiple_of(p * wide, 128), wide)].reshape(fr, wide)
        h = (xb.astype(F32) + project(att, w1o, w2o, w3o)).astype(BF16)
        hid[p] = h
        h32 = h.astype(F32)
        swp[p + 1] = pltpu.roll(h32, chans, 1).astype(BF16)
        for f in range(2):
            rowf[0, pl.ds(f * pairs + p, 1), :] = h32[f * rows:f * rows + 1]
            rowf[1, pl.ds(f * pairs + p, 1), :] = h32[(f + 1) * rows - 1:(f + 1) * rows]
        return carry

    lax.fori_loop(0, pairs, attend, 0)

    def c_copy(s):
        lanes = pl.ds(256, 384) if s == 0 else pl.ds(0, 384)
        return pltpu.make_async_remote_copy(
            src_ref=swp.at[1 if s == 0 else pairs, :, lanes],
            dst_ref=swp.at[pairs + 1 if s == 0 else 0, :, lanes],
            send_sem=c_send.at[s], recv_sem=c_recv.at[1 - s],
            device_id=(me_t, me_r, me_c + step[s]), device_id_type=MESH,
        )

    def r_copy(s):
        return pltpu.make_async_remote_copy(
            src_ref=rows_out.at[s], dst_ref=rows_in.at[1 - s],
            send_sem=r_send.at[s], recv_sem=r_recv.at[1 - s],
            device_id=(me_t, me_r + step[s], me_c), device_id_type=MESH,
        )

    def d_copy(i):
        return pltpu.make_async_remote_copy(
            src_ref=rows_out.at[i // 2], dst_ref=corn_in.at[3 - i],
            send_sem=d_send.at[i], recv_sem=d_recv.at[3 - i],
            device_id=diag[i][1], device_id_type=MESH,
        )

    rows_out[...] = rowf[...].astype(BF16)
    for s in range(2):
        @pl.when(has_r[s])
        def _():
            r_copy(s).start()
    for i in range(4):
        @pl.when(diag[i][0])
        def _():
            d_copy(i).start()
    for s in range(2):
        @pl.when(has_c[s])
        def _():
            c_copy(s).start()
    for s in range(2):
        @pl.when(has_c[s])
        def _():
            c_copy(1 - s).wait_recv()
        @pl.when(has_r[s])
        def _():
            r_copy(1 - s).wait_recv()
    for i in range(4):
        @pl.when(diag[i][0])
        def _():
            d_copy(3 - i).wait_recv()

    n_rows = rows_in.shape[1]
    pair_at = lax.broadcasted_iota(jnp.int32, (n_rows, 1), 0) % pairs
    first_half = lax.broadcasted_iota(jnp.int32, (1, wide), 1) < chans
    for s in range(2):
        line = rows_in[s].astype(F32)
        turned = pltpu.roll(line, chans, 1)
        left_c = pltpu.roll(corn_in[2 * s].astype(F32), chans, 1)
        right_c = pltpu.roll(corn_in[2 * s + 1].astype(F32), chans, 1)
        before = jnp.where(
            pair_at == 0, pltpu.roll(left_c, n_rows - (pairs - 1), 0), pltpu.roll(turned, 1, 0)
        )
        after = jnp.where(
            pair_at == pairs - 1,
            pltpu.roll(right_c, pairs - 1, 0),
            pltpu.roll(turned, n_rows - 1, 0),
        )
        tap = 6 * s
        edge[s] = (
            jnp.where(first_half, before, turned) * taps[tap:tap + 1]
            + line * taps[tap + 1:tap + 2]
            + jnp.where(first_half, turned, after) * taps[tap + 2:tap + 3]
        )

    row_at = lax.broadcasted_iota(jnp.int32, (rows, 1), 0)

    def convolve(p, carry):
        for f in range(2):
            at = pl.ds(f * rows, rows)
            h = hid[p, at].astype(F32)
            sw = swp[p + 1, at].astype(F32)
            mid_b = jnp.where(lane < 64, swp[p, at, 256:384].astype(F32), sw[:, 256:384])
            left = jnp.concatenate([swp[p, at, 0:256].astype(F32), mid_b, sw[:, 384:640]], 1)
            mid_a = jnp.where(lane < 64, sw[:, 256:384], swp[p + 2, at, 256:384].astype(F32))
            right = jnp.concatenate([sw[:, 0:256], mid_a, swp[p + 2, at, 384:640].astype(F32)], 1)
            acc = []
            for a in range(3):
                acc.append(
                    left * taps[3 * a:3 * a + 1]
                    + h * taps[3 * a + 1:3 * a + 2]
                    + right * taps[3 * a + 2:3 * a + 3]
                )
            above = edge[0, pl.ds(f * pairs + p, 1), :]
            below = edge[1, pl.ds(f * pairs + p, 1), :]
            down = jnp.where(row_at == 0, above, pltpu.roll(acc[0], 1, 0))
            up = jnp.where(row_at == rows - 1, below, pltpu.roll(acc[2], rows - 1, 0))
            res = (h + acc[1]) + (down + up)
            out_ref[f, :, pl.ds(pl.multiple_of(p * wide, 128), wide)] = res.astype(BF16)
        return carry

    lax.fori_loop(0, pairs, convolve, 0)

    for s in range(2):
        @pl.when(has_t[s])
        def _():
            def done(p, carry):
                t_copy(s, p).wait_send()
                return carry
            lax.fori_loop(0, pairs, done, 0)
        @pl.when(has_c[s])
        def _():
            c_copy(s).wait_send()
        @pl.when(has_r[s])
        def _():
            r_copy(s).wait_send()
    for i in range(4):
        @pl.when(diag[i][0])
        def _():
            d_copy(i).wait_send()


def body(sizes, latents, w_qkv, w_out, conv_weight):
    frames, rows, merged = latents.shape
    chans = w_out.shape[0]
    wide = 2 * chans
    pairs = merged // wide
    fr = frames * rows
    lines = -(-frames * pairs // 16) * 16
    vmem = pltpu.VMEM
    dma = pltpu.SemaphoreType.DMA
    scratch = [
        vmem((pairs, 3, fr, wide), BF16),
        vmem((pairs, fr, wide), BF16),
        vmem((pairs, 3, fr, wide), BF16),
        vmem((pairs, 3, fr, wide), BF16),
        vmem((pairs, fr, wide), BF16),
        vmem((pairs + 2, fr, wide), BF16),
        vmem((2, lines, wide), F32),
        vmem((2, lines, wide), BF16),
        vmem((2, lines, wide), BF16),
        vmem((4, lines, wide), BF16),
        vmem((2, lines, wide), F32),
        vmem((384, 256), BF16), vmem((wide, 128), BF16), vmem((384, 256), BF16),
        vmem((384, 512), BF16), vmem((wide, 256), BF16), vmem((384, 512), BF16),
        vmem((384, 256), BF16), vmem((wide, 128), BF16), vmem((384, 256), BF16),
        vmem((9, wide), F32),
        vmem((wide, 256), BF16),
        vmem((256, 256), BF16),
        dma((2, pairs)), dma((2, pairs)),
        dma((2,)), dma((2,)), dma((2,)), dma((2,)), dma((4,)), dma((4,)),
    ]
    cells = frames * rows * merged // chans
    return pl.pallas_call(
        functools.partial(kernel, sizes),
        out_shape=jax.ShapeDtypeStruct(latents.shape, BF16),
        in_specs=[pl.BlockSpec(memory_space=vmem)] * 4,
        out_specs=pl.BlockSpec(memory_space=vmem),
        scratch_shapes=scratch,
        compiler_params=pltpu.CompilerParams(
            collective_id=0, has_side_effects=True, vmem_limit_bytes=48 * 2**20
        ),
        cost_estimate=pl.CostEstimate(
            flops=2 * cells * chans * chans * 8, bytes_accessed=4 * cells * chans,
            transcendentals=cells * 25,
        ),
    )(latents, w_qkv, w_out, conv_weight)


def solution(mesh):
    sizes = tuple(mesh.shape[name] for name in ("tm", "row", "col"))
    placed = (P("tm", "row", "col"), P(), P(), P())
    return jax.shard_map(
        functools.partial(body, sizes), mesh=mesh, in_specs=placed,
        out_specs=P("tm", "row", "col"), check_vma=False,
    )
```

time: 89.1 us -> 26.1 us (0.29)
  the two profiles are of different devices: /device:TPU:10 before, /device:TPU:0 now
where the time goes in v1:
time: 26.1 us; the launch traced here: 25.9 us
  Pallas kernels  21.1 us (81%)
  local copies, waits for them, and re-layouts  4.69 us (18%)
    pallas_call x1, Pallas kernels, body(): pl.pallas_call(functools.partial(kernel, sizes), out_shape=jax.ShapeDtype...  21.1 us
    unnamed x9, local copies, waits for them, and re-layouts  4.69 us

profile of v1, /device:TPU:0, one launch (start us, length us, event | category | flops | bytes accessed | tf_op | source)
XLA Modules:
  0.0 25.9 jit_solution(8927844577814545582)
XLA Ops:
  0.0 0.0 copy-start
  0.0 1.1 %copy-done = bf16[2,32,5120]{2,1,0:T(8,128)(2,1)S(1)} copy-done((bf16[2,32,5120]{2,1,0:T(8,128)(2,1)S(1)}, bf16[2,32,5120]{2,1,0:T(8,128)(2,1)}, u32[]{:S(2)}) %copy-start) | copy-done | bytes 655384
  1.1 0.0 copy-start.1
  1.1 1.1 %copy-done.1 = bf16[320,960]{1,0:T(8,128)(2,1)S(1)} copy-done((bf16[320,960]{1,0:T(8,128)(2,1)S(1)}, bf16[320,960]{1,0:T(8,128)(2,1)}, u32[]{:S(2)}) %copy-start.1) | copy-done | bytes 614424
  2.2 0.0 copy-start.2
  2.2 0.9 %copy-done.2 = bf16[320,320]{1,0:T(8,128)(2,1)S(1)} copy-done((bf16[320,320]{1,0:T(8,128)(2,1)S(1)}, bf16[320,320]{1,0:T(8,128)(2,1)}, u32[]{:S(2)}) %copy-start.2) | copy-done | bytes 204824
  3.1 0.0 copy-start.3
  3.1 0.7 %copy-done.3 = f32[9,320]{1,0:T(8,128)S(1)} copy-done((f32[9,320]{1,0:T(8,128)S(1)}, f32[9,320]{1,0:T(8,128)}, u32[]{:S(2)}) %copy-start.3) | copy-done | bytes 11544
  3.9 21.1 %shard_map.46 = bf16[2,32,5120]{2,1,0:T(8,128)(2,1)S(1)} custom-call(bf16[2,32,5120]{2,1,0:T(8,128)(2,1)S(1)} %copy-done, bf16[320,960]{1,0:T(8,128)(2,1)S(1)} %copy-done.1, bf16[320,320]{1,0:T(8,128)(2,1)S(1)} %copy-done.2, f32[9,320]{1,0:T(8,128)S(1)} %copy-done.3), custom_call_target="tpu_custom_call" | custom-call | flops 1677721600 | bytes 1310720 | tf_op jit(solution)/shard_map/pallas_call | solution.py:359
  25.0 0.8 %copy.6 = bf16[2,32,5120]{2,1,0:T(8,128)(2,1)} copy(bf16[2,32,5120]{2,1,0:T(8,128)(2,1)S(1)} %shard_map.46) | data formatting | bytes 1310720
Async XLA Ops:
  0.0 1.1 %copy-start = (bf16[2,32,5120]{2,1,0:T(8,128)(2,1)S(1)}, bf16[2,32,5120]{2,1,0:T(8,128)(2,1)}, u32[]{:S(2)}) copy-start(bf16[2,32,5120]{2,1,0:T(8,128)(2,1)} %x_ref.1) | copy-start | bytes 1966084
  1.1 1.1 %copy-start.1 = (bf16[320,960]{1,0:T(8,128)(2,1)S(1)}, bf16[320,960]{1,0:T(8,128)(2,1)}, u32[]{:S(2)}) copy-start(bf16[320,960]{1,0:T(8,128)(2,1)} %wqkv_ref.1) | copy-start | bytes 1843204
  2.2 0.9 %copy-start.2 = (bf16[320,320]{1,0:T(8,128)(2,1)S(1)}, bf16[320,320]{1,0:T(8,128)(2,1)}, u32[]{:S(2)}) copy-start(bf16[320,320]{1,0:T(8,128)(2,1)} %wout_ref.1) | copy-start | bytes 614404
  3.1 0.7 %copy-start.3 = (f32[9,320]{1,0:T(8,128)S(1)}, f32[9,320]{1,0:T(8,128)}, u32[]{:S(2)}) copy-start(f32[9,320]{1,0:T(8,128)} %cw_ref.1) | copy-start | bytes 34564

commit v2 on v1

--- a/solution.py
+++ b/solution.py
@@ -24,12 +24,21 @@
 
 def kernel(
     sizes,
-    x_ref, wqkv_ref, wout_ref, cw_ref, out_ref,
-    norm, q_s, k_s, v_s, hid, swp, rowf, rows_out, rows_in, corn_in, edge,
+    x_hbm, wqkv_hbm, wout_hbm, cw_hbm, out_ref,
+    x_ref, wqkv_ref, wout_ref, cw_ref, acc_s,
+    cells_in, q_s, k_s, v_s, hid, swp, rowf, rows_out, rows_in, corn_in, edge,
     w1q, w2q, w3q, w1kv, w2kv, w3kv, w1o, w2o, w3o, taps, ones2, heads,
-    t_send, t_recv, c_send, c_recv, r_send, r_recv, d_send, d_recv,
+    t_send, t_recv, c_send, c_recv, r_send, r_recv, d_send, d_recv, load,
 ):
     n_t, n_r, n_c = sizes
+    loads = [
+        pltpu.make_async_copy(src, dst, load.at[i])
+        for i, (src, dst) in enumerate(
+            ((x_hbm, x_ref), (wqkv_hbm, wqkv_ref), (wout_hbm, wout_ref), (cw_hbm, cw_ref))
+        )
+    ]
+    for copy in loads:
+        copy.start()
     frames, rows, merged = x_ref.shape
     chans = wout_ref.shape[0]
     wide = 2 * chans
@@ -60,6 +69,28 @@
             pl.semaphore_signal(barrier, inc=1, device_id=where, device_id_type=MESH)
         count = count + jnp.where(ok, 1, 0).astype(jnp.int32)
 
+    pl.semaphore_wait(barrier, count)
+
+    def t_copy(s, p):
+        return pltpu.make_async_remote_copy(
+            src_ref=x_hbm.at[:, :, pl.ds(pl.multiple_of(p * wide, 128), wide)],
+            dst_ref=cells_in.at[p, 1 - s],
+            send_sem=t_send.at[s, p], recv_sem=t_recv.at[1 - s, p],
+            device_id=(me_t + step[s], me_r, me_c), device_id_type=MESH,
+        )
+
+    def turn(k):
+        return jnp.where(k == 0, 0, jnp.where(k == 1, pairs - 1, k - 1))
+
+    def send(k, carry):
+        for s in range(2):
+            @pl.when(has_t[s])
+            def _():
+                t_copy(s, turn(k)).start()
+        return carry
+
+    lax.fori_loop(0, pairs, send, 0)
+
     lane = lax.broadcasted_iota(jnp.int32, (1, 128), 1)
 
     at = lax.broadcasted_iota(jnp.int32, (wide, 256), 0)
@@ -72,7 +103,7 @@
     for s in range(2):
         @pl.when(jnp.logical_not(has_t[s]))
         def _():
-            norm[:, s] = jnp.zeros((pairs, fr, wide), BF16)
+            cells_in[:, s] = jnp.zeros((pairs, frames, rows, wide), BF16)
         @pl.when(jnp.logical_not(has_c[s]))
         def _():
             swp[0 if s == 0 else pairs + 1] = jnp.zeros((fr, wide), BF16)
@@ -84,29 +115,18 @@
         def _():
             corn_in[i] = jnp.zeros(corn_in.shape[1:], BF16)
 
-    pl.semaphore_wait(barrier, count)
-
-    def t_copy(s, p):
-        return pltpu.make_async_remote_copy(
-            src_ref=norm.at[p, 2], dst_ref=norm.at[p, 1 - s],
-            send_sem=t_send.at[s, p], recv_sem=t_recv.at[1 - s, p],
-            device_id=(me_t + step[s], me_r, me_c), device_id_type=MESH,
-        )
-
-    def normalise(p, carry):
-        xb = x_ref[:, :, pl.ds(pl.multiple_of(p * wide, 128), wide)].reshape(fr, wide)
+    def normalise(xb):
         sums = dot(xb, ones2[...]) * (1.0 / chans)
         cent = xb.astype(F32) - widen(sums[:, :128], sums[:, 128:], lane)
         var = dot((cent * cent).astype(BF16), ones2[...]) * (1.0 / chans)
         inv = lax.rsqrt(var + 1e-05)
-        norm[p, 2] = (cent * widen(inv[:, :128], inv[:, 128:], lane)).astype(BF16)
-        for s in range(2):
-            @pl.when(has_t[s])
-            def _():
-                t_copy(s, p).start()
-        return carry
-
-    lax.fori_loop(0, pairs, normalise, 0)
+        return (cent * widen(inv[:, :128], inv[:, 128:], lane)).astype(BF16)
+
+    def mine(p):
+        return x_ref[:, :, pl.ds(pl.multiple_of(p * wide, 128), wide)].reshape(fr, wide)
+
+    for copy in loads[1:]:
+        copy.wait()
 
     pad = wide - chans - 256
     def split(w32, r1, r2, r3, lo1, lo2):
@@ -137,10 +157,11 @@
         vals = jnp.concatenate([o1[:, 256:], o2[:, 128:], o3[:, 256:]], 1)
         return keys, vals
 
+    loads[0].wait()
     group = 2
     def own(g, carry):
         at = pl.ds(g * group, group)
-        a = norm[at, 2].reshape(group * fr, wide)
+        a = jnp.concatenate([normalise(mine(g * group + i)) for i in range(group)], 0)
         q = project(a, w1q, w2q, w3q) * (HEAD_DIM ** -0.5 * LOG2E)
         q_s[at] = q.astype(BF16).reshape(group, fr, wide)
         keys, vals = keys_values(a)
@@ -157,12 +178,22 @@
         slot = (0, 2, 1)[w // 2]
         return slot, (w % 2) * rows
 
-    def attend(p, carry):
+    def c_copy(s):
+        lanes = pl.ds(256, 384) if s == 0 else pl.ds(0, 384)
+        return pltpu.make_async_remote_copy(
+            src_ref=swp.at[1 if s == 0 else pairs, :, lanes],
+            dst_ref=swp.at[pairs + 1 if s == 0 else 0, :, lanes],
+            send_sem=c_send.at[s], recv_sem=c_recv.at[1 - s],
+            device_id=(me_t, me_r, me_c + step[s]), device_id_type=MESH,
+        )
+
+    def attend(k, carry):
+        p = turn(k)
         for s in range(2):
             @pl.when(has_t[s])
             def _():
                 t_copy(1 - s, p).wait_recv()
-        keys, vals = keys_values(norm[p, 0:2].reshape(2 * fr, wide))
+        keys, vals = keys_values(normalise(cells_in[p].reshape(2 * fr, wide)))
         k_s[p, 0:2] = keys.reshape(2, fr, wide)
         v_s[p, 0:2] = vals.reshape(2, fr, wide)
         outs = []
@@ -195,26 +226,20 @@
                 mixes.append((mixed / total).astype(BF16))
             outs.append(jnp.concatenate(mixes, 0))
         att = jnp.concatenate(outs, 1)
-        xb = x_ref[:, :, pl.ds(pl.multiple_of(p * wide, 128), wide)].reshape(fr, wide)
-        h = (xb.astype(F32) + project(att, w1o, w2o, w3o)).astype(BF16)
+        h = (mine(p).astype(F32) + project(att, w1o, w2o, w3o)).astype(BF16)
         hid[p] = h
         h32 = h.astype(F32)
         swp[p + 1] = pltpu.roll(h32, chans, 1).astype(BF16)
         for f in range(2):
             rowf[0, pl.ds(f * pairs + p, 1), :] = h32[f * rows:f * rows + 1]
             rowf[1, pl.ds(f * pairs + p, 1), :] = h32[(f + 1) * rows - 1:(f + 1) * rows]
+        for s in range(2):
+            @pl.when(has_c[s] & (k == s))
+            def _():
+                c_copy(s).start()
         return carry
 
     lax.fori_loop(0, pairs, attend, 0)
-
-    def c_copy(s):
-        lanes = pl.ds(256, 384) if s == 0 else pl.ds(0, 384)
-        return pltpu.make_async_remote_copy(
-            src_ref=swp.at[1 if s == 0 else pairs, :, lanes],
-            dst_ref=swp.at[pairs + 1 if s == 0 else 0, :, lanes],
-            send_sem=c_send.at[s], recv_sem=c_recv.at[1 - s],
-            device_id=(me_t, me_r, me_c + step[s]), device_id_type=MESH,
-        )
 
     def r_copy(s):
         return pltpu.make_async_remote_copy(
@@ -242,41 +267,7 @@
     for s in range(2):
         @pl.when(has_c[s])
         def _():
-            c_copy(s).start()
-    for s in range(2):
-        @pl.when(has_c[s])
-        def _():
             c_copy(1 - s).wait_recv()
-        @pl.when(has_r[s])
-        def _():
-            r_copy(1 - s).wait_recv()
-    for i in range(4):
-        @pl.when(diag[i][0])
-        def _():
-            d_copy(3 - i).wait_recv()
-
-    n_rows = rows_in.shape[1]
-    pair_at = lax.broadcasted_iota(jnp.int32, (n_rows, 1), 0) % pairs
-    first_half = lax.broadcasted_iota(jnp.int32, (1, wide), 1) < chans
-    for s in range(2):
-        line = rows_in[s].astype(F32)
-        turned = pltpu.roll(line, chans, 1)
-        left_c = pltpu.roll(corn_in[2 * s].astype(F32), chans, 1)
-        right_c = pltpu.roll(corn_in[2 * s + 1].astype(F32), chans, 1)
-        before = jnp.where(
-            pair_at == 0, pltpu.roll(left_c, n_rows - (pairs - 1), 0), pltpu.roll(turned, 1, 0)
-        )
-        after = jnp.where(
-            pair_at == pairs - 1,
-            pltpu.roll(right_c, pairs - 1, 0),
-            pltpu.roll(turned, n_rows - 1, 0),
-        )
-        tap = 6 * s
-        edge[s] = (
-            jnp.where(first_half, before, turned) * taps[tap:tap + 1]
-            + line * taps[tap + 1:tap + 2]
-            + jnp.where(first_half, turned, after) * taps[tap + 2:tap + 3]
-        )
 
     row_at = lax.broadcasted_iota(jnp.int32, (rows, 1), 0)
 
@@ -296,15 +287,56 @@
                     + h * taps[3 * a + 1:3 * a + 2]
                     + right * taps[3 * a + 2:3 * a + 3]
                 )
+            down = jnp.where(row_at == 0, 0.0, pltpu.roll(acc[0], 1, 0))
+            up = jnp.where(row_at == rows - 1, 0.0, pltpu.roll(acc[2], rows - 1, 0))
+            acc_s[p, f] = (h + acc[1]) + (down + up)
+        return carry
+
+    lax.fori_loop(0, pairs, convolve, 0)
+
+    for s in range(2):
+        @pl.when(has_r[s])
+        def _():
+            r_copy(1 - s).wait_recv()
+    for i in range(4):
+        @pl.when(diag[i][0])
+        def _():
+            d_copy(3 - i).wait_recv()
+
+    n_rows = rows_in.shape[1]
+    pair_at = lax.broadcasted_iota(jnp.int32, (n_rows, 1), 0) % pairs
+    first_half = lax.broadcasted_iota(jnp.int32, (1, wide), 1) < chans
+    for s in range(2):
+        line = rows_in[s].astype(F32)
+        turned = pltpu.roll(line, chans, 1)
+        left_c = pltpu.roll(corn_in[2 * s].astype(F32), chans, 1)
+        right_c = pltpu.roll(corn_in[2 * s + 1].astype(F32), chans, 1)
+        before = jnp.where(
+            pair_at == 0, pltpu.roll(left_c, n_rows - (pairs - 1), 0), pltpu.roll(turned, 1, 0)
+        )
+        after = jnp.where(
+            pair_at == pairs - 1,
+            pltpu.roll(right_c, pairs - 1, 0),
+            pltpu.roll(turned, n_rows - 1, 0),
+        )
+        tap = 6 * s
+        edge[s] = (
+            jnp.where(first_half, before, turned) * taps[tap:tap + 1]
+            + line * taps[tap + 1:tap + 2]
+            + jnp.where(first_half, turned, after) * taps[tap + 2:tap + 3]
+        )
+
+    def finish(p, carry):
+        for f in range(2):
             above = edge[0, pl.ds(f * pairs + p, 1), :]
             below = edge[1, pl.ds(f * pairs + p, 1), :]
-            down = jnp.where(row_at == 0, above, pltpu.roll(acc[0], 1, 0))
-            up = jnp.where(row_at == rows - 1, below, pltpu.roll(acc[2], rows - 1, 0))
-            res = (h + acc[1]) + (down + up)
+            head = acc_s[p, f, 0:8] + jnp.where(row_at[0:8] == 0, above, 0.0)
+            foot = acc_s[p, f, rows - 8:] + jnp.where(row_at[rows - 8:] == rows - 1, below, 0.0)
+            res = jnp.concatenate([head, acc_s[p, f, 8:rows - 8], foot], 0)
             out_ref[f, :, pl.ds(pl.multiple_of(p * wide, 128), wide)] = res.astype(BF16)
         return carry
 
-    lax.fori_loop(0, pairs, convolve, 0)
+    lax.fori_loop(0, pairs, finish, 0)
 
     for s in range(2):
         @pl.when(has_t[s])
@@ -335,7 +367,10 @@
     vmem = pltpu.VMEM
     dma = pltpu.SemaphoreType.DMA
     scratch = [
-        vmem((pairs, 3, fr, wide), BF16),
+        vmem(latents.shape, BF16), vmem(w_qkv.shape, BF16),
+        vmem(w_out.shape, BF16), vmem(conv_weight.shape, F32),
+        vmem((pairs, frames, rows, wide), F32),
+        vmem((pairs, 2, frames, rows, wide), BF16),
         vmem((pairs, fr, wide), BF16),
         vmem((pairs, 3, fr, wide), BF16),
         vmem((pairs, 3, fr, wide), BF16),
@@ -353,17 +388,17 @@
         vmem((wide, 256), BF16),
         vmem((256, 256), BF16),
         dma((2, pairs)), dma((2, pairs)),
-        dma((2,)), dma((2,)), dma((2,)), dma((2,)), dma((4,)), dma((4,)),
+        dma((2,)), dma((2,)), dma((2,)), dma((2,)), dma((4,)), dma((4,)), dma((4,)),
     ]
     cells = frames * rows * merged // chans
     return pl.pallas_call(
         functools.partial(kernel, sizes),
         out_shape=jax.ShapeDtypeStruct(latents.shape, BF16),
-        in_specs=[pl.BlockSpec(memory_space=vmem)] * 4,
+        in_specs=[pl.BlockSpec(memory_space=pl.ANY)] * 4,
         out_specs=pl.BlockSpec(memory_space=vmem),
         scratch_shapes=scratch,
         compiler_params=pltpu.CompilerParams(
-            collective_id=0, has_side_effects=True, vmem_limit_bytes=48 * 2**20
+            collective_id=0, has_side_effects=True, vmem_limit_bytes=56 * 2**20
         ),
         cost_estimate=pl.CostEstimate(
             flops=2 * cells * chans * chans * 8, bytes_accessed=4 * cells * chans,

time: 26.1 us -> 25.1 us (0.962)
  local copies, waits for them, and re-layouts: 4.69 us -> 1.97 us
  Pallas kernels: 21.1 us -> 23 us
    unnamed x9 -> x1, local copies, waits for them, and re-layouts: 4.69 us -> 1.97 us
    pallas_call x1, Pallas kernels: 21.1 us -> 23 us  [body(): pl.pallas_call(functools.partial(kernel, sizes), out_shape=jax.ShapeDtype...]
where the time goes in v2:
time: 25.1 us; the launch traced here: 25 us
  Pallas kernels  23 us (92%)
  local copies, waits for them, and re-layouts  1.97 us (8%)
    pallas_call x1, Pallas kernels, body(): pl.pallas_call(functools.partial(kernel, sizes), out_shape=jax.ShapeDtype...  23 us
    unnamed x1, local copies, waits for them, and re-layouts  1.97 us

profile of v2, /device:TPU:0, one launch (start us, length us, event | category | flops | bytes accessed | tf_op | source)
XLA Modules:
  0.0 25.0 jit_solution(15667074491997012935)
XLA Ops:
  0.0 23.0 %shard_map.46 = bf16[2,32,5120]{2,1,0:T(8,128)(2,1)} custom-call(bf16[2,32,5120]{2,1,0:T(8,128)(2,1)} %x_hbm.1, bf16[320,960]{1,0:T(8,128)(2,1)} %wqkv_hbm.1, bf16[320,320]{1,0:T(8,128)(2,1)} %wout_hbm.1, f32[9,320]{1,0:T(8,128)} %cw_hbm.1), custom_call_target="tpu_custom_call" | custom-call | flops 1677721600 | bytes 1310720 | tf_op jit(solution)/shard_map/pallas_call | solution.py:394
  23.0 2.0 %copy.6 = bf16[2,32,5120]{2,1,0:T(8,128)(2,1)} copy(bf16[2,32,5120]{2,1,0:T(8,128)(2,1)} %shard_map.46) | data formatting | bytes 1310720

commit v3 on v2

--- a/solution.py
+++ b/solution.py
@@ -398,7 +398,7 @@
         out_specs=pl.BlockSpec(memory_space=vmem),
         scratch_shapes=scratch,
         compiler_params=pltpu.CompilerParams(
-            collective_id=0, has_side_effects=True, vmem_limit_bytes=56 * 2**20
+            collective_id=0, has_side_effects=True, vmem_limit_bytes=53 * 2**20
         ),
         cost_estimate=pl.CostEstimate(
             flops=2 * cells * chans * chans * 8, bytes_accessed=4 * cells * chans,

time: 25.1 us -> 24.9 us (level)
  Pallas kernels: 23 us -> 22.2 us
  local copies, waits for them, and re-layouts: 1.97 us -> 2.52 us
    pallas_call x1, Pallas kernels: 23 us -> 22.2 us  [body(): pl.pallas_call(functools.partial(kernel, sizes), out_shape=jax.ShapeDtype...]
    unnamed x1 -> x5, local copies, waits for them, and re-layouts: 1.97 us -> 2.52 us
where the time goes in v3:
time: 24.9 us; the launch traced here: 24.7 us
  Pallas kernels  22.2 us (89%)
  local copies, waits for them, and re-layouts  2.52 us (10%)
    pallas_call x1, Pallas kernels, body(): pl.pallas_call(functools.partial(kernel, sizes), out_shape=jax.ShapeDtype...  22.2 us
    unnamed x5, local copies, waits for them, and re-layouts  2.52 us

profile of v3, /device:TPU:0, one launch (start us, length us, event | category | flops | bytes accessed | tf_op | source)
XLA Modules:
  0.0 24.7 jit_solution(9328989416877493482)
XLA Ops:
  0.0 0.0 copy-start
  0.0 0.9 %copy-done = bf16[320,320]{1,0:T(8,128)(2,1)S(1)} copy-done((bf16[320,320]{1,0:T(8,128)(2,1)S(1)}, bf16[320,320]{1,0:T(8,128)(2,1)}, u32[]{:S(2)}) %copy-start) | copy-done | bytes 204824
  0.9 0.0 copy-start.1
  0.9 0.7 %copy-done.1 = f32[9,320]{1,0:T(8,128)S(1)} copy-done((f32[9,320]{1,0:T(8,128)S(1)}, f32[9,320]{1,0:T(8,128)}, u32[]{:S(2)}) %copy-start.1) | copy-done | bytes 11544
  1.7 22.2 %shard_map.46 = bf16[2,32,5120]{2,1,0:T(8,128)(2,1)S(1)} custom-call(bf16[2,32,5120]{2,1,0:T(8,128)(2,1)} %x_hbm.1, bf16[320,960]{1,0:T(8,128)(2,1)} %wqkv_hbm.1, bf16[320,320]{1,0:T(8,128)(2,1)S(1)} %copy-done, f32[9,320]{1,0:T(8,128)S(1)} %copy-done.1), custom_call_target="tpu_custom_call" | custom-call | flops 1677721600 | bytes 1310720 | tf_op jit(solution)/shard_map/pallas_call | solution.py:394
  23.9 0.8 %copy.6 = bf16[2,32,5120]{2,1,0:T(8,128)(2,1)} copy(bf16[2,32,5120]{2,1,0:T(8,128)(2,1)S(1)} %shard_map.46) | data formatting | bytes 1310720
Async XLA Ops:
  0.0 0.9 %copy-start = (bf16[320,320]{1,0:T(8,128)(2,1)S(1)}, bf16[320,320]{1,0:T(8,128)(2,1)}, u32[]{:S(2)}) copy-start(bf16[320,320]{1,0:T(8,128)(2,1)} %wout_hbm.1) | copy-start | bytes 614404
  0.9 0.7 %copy-start.1 = (f32[9,320]{1,0:T(8,128)S(1)}, f32[9,320]{1,0:T(8,128)}, u32[]{:S(2)}) copy-start(f32[9,320]{1,0:T(8,128)} %cw_hbm.1) | copy-start | bytes 34564
